TPU v7x, 32 devices: a whole 2x2x4 slice. The times are simulated.
32 devices in a mesh: groups: 2 (over y), seq: 4 (over z), fam: 2 (over x), head: 2 (over core).
Axes of the slice: x: 2, y: 2, z: 4, core: 2. Of those that a mesh axis runs over, the one named last changes fastest.
Arguments:
- blocks: bfloat16 [16, 4, 128, 768], P(('groups', 'seq', 'fam'), None, None, 'head'), parts along dimension 0, may hold values from -6 to 6
- cotangent: bfloat16 [16, 4, 128, 768], P(('groups', 'seq', 'fam'), None, None, 'head'), parts along dimension 0, may hold values from -6 to 6
- w_query: bfloat16 [768, 768], P(None, 'head'), may hold values from -0.21875 to 0.21875
- w_key: bfloat16 [768, 768], P(None, 'head'), may hold values from -0.21875 to 0.21875
- w_value: bfloat16 [768, 768], P(None, 'head'), may hold values from -0.21875 to 0.21875
- w_out: bfloat16 [768, 768], P(None, 'head'), may hold values from -0.21875 to 0.21875
- block_family: int32 [16], P('groups'), parts along dimension 0, may hold values from 0 to 3, as said below
- family_depth: int32 [8], P('groups'), parts along dimension 0, may hold values from 1 to 20, as said below
Outputs:
- layer_out: bfloat16 [16, 4, 128, 768], P(('groups', 'seq', 'fam'), None, None, 'head'), parts along dimension 0
- input_grad: bfloat16 [16, 4, 128, 768], P(('groups', 'seq', 'fam'), None, None, 'head'), parts along dimension 0
- weight_grad: float32 [1536, 2, 768], P(('groups', 'seq', 'fam'), None, 'head'), parts along dimension 0
There are 2 independent parts, one for each index of `groups`. A program takes and returns all parts, laid end to end along the dimension named above; an argument that names none is the same for every part. Nothing has to cross between parts.
Inputs may be any that keep to these rules, and one draw needn't show every extreme that they name: `block_family`: family numbers never fall along the blocks, and each of the 4 families holds at least one block. `family_depth`: A family that holds n blocks has a depth above (n - 1) * 4 and at most n * 4; one family holds 5 blocks.
All inputs are finite; a program needn't handle non-finite values.
Results may differ from a plain program's by a relative error of at most 0.011.
Values may be sent and summed in bfloat16 or wider, within the bound.
A program may use at most 64 MiB of HBM per device.

v0:
```python
import jax
import jax.numpy as jnp
from jax import lax
from jax.sharding import PartitionSpec as P

D = 768
H = 12
F = 4


def tied_total(partial_value, family):
    slots = (jnp.arange(F, dtype=jnp.int32) == family).astype(jnp.float32)[
        :, None, None, None
    ] * partial_value[None]
    table = lax.psum(slots, ("seq", "fam"))
    return lax.dynamic_index_in_dim(table, family, 0, keepdims=False)


def shards(blocks, cotangent, w_query, w_key, w_value, w_out, block_family, family_depth):
    head_size = D // H
    local_heads = w_query.shape[1] // head_size
    block_rows = blocks.shape[0] * blocks.shape[1]
    columns = blocks.shape[2]
    full_blocks = lax.all_gather(blocks, "head", axis=3, tiled=True)
    flat_tokens = full_blocks.reshape(-1, D)

    def project(weight):
        return jnp.dot(flat_tokens, weight, preferred_element_type=jnp.float32).astype(jnp.bfloat16)

    shape_four = (block_rows, columns, local_heads, head_size)
    query_rows = project(w_query).reshape(shape_four)
    key_rows = project(w_key).reshape(shape_four)
    value_rows = project(w_value).reshape(shape_four)
    my_block = lax.axis_index(("seq", "fam"))
    family = block_family[my_block]
    family_first = jnp.sum((block_family < family).astype(jnp.int32))
    depth = family_depth[family]
    row_place = (my_block - family_first) * block_rows + jnp.arange(block_rows, dtype=jnp.int32)
    row_mask = (row_place < depth).astype(jnp.float32)
    mask_four = row_mask[:, None, None, None]
    logit_scale = 1.0 / (jnp.sqrt(jnp.float32(head_size)) * jnp.sqrt(depth.astype(jnp.float32)))
    masked_query = query_rows * mask_four.astype(jnp.bfloat16)
    partial_logits = jnp.einsum(
        "rihd,rjhd->hij", masked_query, key_rows, preferred_element_type=jnp.float32
    )
    logits = tied_total(partial_logits, family) * logit_scale
    expo = jnp.exp(logits)
    attention = expo / jnp.sum(expo, axis=-1, keepdims=True)
    attention_b16 = attention.astype(jnp.bfloat16)
    mixed = jnp.einsum(
        "hij,rjhd->rihd", attention_b16, value_rows, preferred_element_type=jnp.float32
    ).astype(jnp.bfloat16)
    mixed_flat = mixed.reshape(-1, local_heads * head_size)
    layer_out = jnp.dot(
        lax.all_gather(mixed_flat, "head", axis=1, tiled=True),
        w_out,
        preferred_element_type=jnp.float32,
    )
    layer_out = layer_out.astype(jnp.bfloat16).reshape(blocks.shape)
    flat_cot = cotangent.reshape(-1, cotangent.shape[3])
    cot_terms = lax.dot_general(
        flat_cot, w_out, (((1,), (1,)), ((), ())), preferred_element_type=jnp.float32
    )
    out_grad = (
        lax.psum_scatter(cot_terms, "head", scatter_dimension=1, tiled=True)
        .astype(jnp.bfloat16)
        .reshape(shape_four)
    )
    partial_grad = jnp.einsum(
        "rihd,rjhd->hij", out_grad, value_rows, preferred_element_type=jnp.float32
    )
    attn_grad = tied_total(partial_grad, family)
    centred = attn_grad - jnp.sum(attention * attn_grad, axis=-1, keepdims=True)
    logit_grad = (logit_scale * attention * centred).astype(jnp.bfloat16)
    query_grad = (
        jnp.einsum("hij,rjhd->rihd", logit_grad, key_rows, preferred_element_type=jnp.float32)
        * mask_four
    ).astype(jnp.bfloat16)
    key_grad = (
        jnp.einsum("hij,rihd->rjhd", logit_grad, query_rows, preferred_element_type=jnp.float32)
        * mask_four
    ).astype(jnp.bfloat16)
    value_grad = jnp.einsum(
        "hij,rihd->rjhd", attention_b16, out_grad, preferred_element_type=jnp.float32
    ).astype(jnp.bfloat16)
    local_width = local_heads * head_size
    query_flat = query_grad.reshape(-1, local_width)
    key_flat = key_grad.reshape(-1, local_width)
    value_flat = value_grad.reshape(-1, local_width)

    def back(grad, weight):
        return lax.dot_general(
            grad, weight, (((1,), (1,)), ((), ())), preferred_element_type=jnp.float32
        )

    grad_terms = back(query_flat, w_query) + back(key_flat, w_key) + back(value_flat, w_value)
    input_grad = (
        lax.psum_scatter(grad_terms, "head", scatter_dimension=1, tiled=True)
        .astype(jnp.bfloat16)
        .reshape(blocks.shape)
    )
    stacked = jnp.concatenate([query_flat, key_flat], axis=1)
    own_rows = D // lax.axis_size(("seq", "fam"))
    weight_grad = lax.psum_scatter(
        lax.dot_general(
            flat_tokens, stacked, (((0,), (0,)), ((), ())), preferred_element_type=jnp.float32
        ),
        ("seq", "fam"),
        scatter_dimension=0,
        tiled=True,
    )
    weight_grad = weight_grad.reshape(own_rows, 2, local_width)
    return (layer_out, input_grad, weight_grad)


def solution(mesh):
    return jax.shard_map(
        shards,
        mesh=mesh,
        in_specs=(
            P(("groups", "seq", "fam"), None, None, "head"),
            P(("groups", "seq", "fam"), None, None, "head"),
            P(None, "head"),
            P(None, "head"),
            P(None, "head"),
            P(None, "head"),
            P("groups"),
            P("groups"),
        ),
        out_specs=(
            P(("groups", "seq", "fam"), None, None, "head"),
            P(("groups", "seq", "fam"), None, None, "head"),
            P(("groups", "seq", "fam"), None, "head"),
        ),
        check_vma=False,
    )
```

profile of v0, /device:TPU:0, one launch (start us, length us, event | category | flops | bytes accessed | tf_op | source)
XLA Modules:
  0.0 268.2 jit_solution(10958691846437648044)
XLA Ops:
  7.2 3.0 %fusion.51 = f32[512,768]{1,0:T(8,128)} fusion(bf16[512,384]{1,0:T(8,128)(2,1)} %bitcast.141, bf16[768,384]{1,0:T(8,128)(2,1)} %param.13), kind=kOutput, calls=%fused_computation.71 | convolution fusion | flops 301989888 | bytes 2555904 | tf_op jit(solution)/shard_map/dot_general | solution.py:61
  12.2 1.3 fusion.40
  14.2 2.4 all_gather.6
  18.4 1.8 convolution_convert_fusion.5
  21.8 0.6 compare_convert_fusion.2
  22.5 0.7 fusion.50
  23.7 1.2 convert_element_type.92
  25.5 2.1 broadcast_multiply_fusion
  28.4 131.3 %all-reduce.3.cloned.1.call-done = (f32[4,6,128,128]{3,2,1,0:T(8,128)}, f32[4,6,128,128]{3,2,1,0:T(8,128)}) async-done(((f32[4,6,128,128]{3,2,1,0:T(8,128)}, f32[4,6,128,128]{3,2,1,0:T(8,128)}), (f32[4,6,128,128]{3,2,1,0:T(8,128)}, f32[4,6,128,128]{3,2,1,0:T(8,128)})) %all-reduce.3.cloned.1.call-update) | async-done | bytes 3145744 | tf_op jit(solution)/shard_map/psum | solution.py:15
  159.7 1.2 fusion.33
  160.9 5.3 %fusion.6 = bf16[4,128,6,64]{1,3,0,2:T(8,128)(2,1)S(1)} fusion(f32[4]{0:T(128)S(1)} %get-tuple-element.15, bf16[4,128,6,64]{1,0,3,2:T(4,128)(2,1)S(1)} %reshape.70, f32[4,6,128,128]{3,2,1,0:T(8,128)} %get-tuple-element.13, s32[]{:T(128)S(6)} %select_n.10, f32[]{:T(128)S(6)} %div.11, f32[4,6,128,128]{3,2,1,0:T(8,128)} %get-tuple-element.12, ...), kind=kOutput, calls=%fused_computation.16 | convolution fusion | flops 51610496 | bytes 2370560 | tf_op jit(solution)/shard_map/hij,rjhd->rihd/dot_general | solution.py:76
  166.2 5.4 %fusion.5 = bf16[4,128,6,64]{1,3,0,2:T(8,128)(2,1)S(1)} fusion(bf16[4,128,6,64]{1,0,3,2:T(4,128)(2,1)S(1)} %reshape.69, f32[4]{0:T(128)S(1)} %get-tuple-element.15, f32[4,6,128,128]{3,2,1,0:T(8,128)} %get-tuple-element.13, s32[]{:T(128)S(6)} %select_n.10, f32[]{:T(128)S(6)} %div.11, f32[4,6,128,128]{3,2,1,0:T(8,128)} %get-tuple-element.12, ...), kind=kOutput, calls=%fused_computation.15 | convolution fusion | flops 51610496 | bytes 2370560 | tf_op jit(solution)/shard_map/hij,rihd->rjhd/dot_general | solution.py:80
  171.6 1.4 fusion.4
  173.9 0.6 fusion.48
  175.6 1.8 add_add_fusion
  177.6 1.9 convolution_bitcast_fusion
  179.5 2.0 copy.58
  181.5 1.5 fusion.3
  183.3 2.4 all_gather.7
  185.7 1.3 convolution_convert_fusion.1
  187.1 1.9 convert_element_type.100
  189.0 70.7 %reduce-scatter.10.cloned.1.call-done = f32[96,768]{1,0:T(8,128)} async-done(((f32[768,768]{1,0:T(8,128)}), f32[96,768]{1,0:T(8,128)}) %reduce-scatter.10.cloned.1.call-update) | async-done | bytes 294928
  259.7 1.1 copy.59
  260.8 0.9 copy.53
  (48 shorter events, 7.1 us)
Async XLA Ops:
  7.2 10.3 %copy-start = (bf16[768,384]{1,0:T(8,128)(2,1)S(1)}, bf16[768,384]{1,0:T(8,128)(2,1)}, u32[]{:S(2)}) copy-start(bf16[768,384]{1,0:T(8,128)(2,1)} %param.10) | copy-start | bytes 1769476
  7.2 16.5 %reduce-scatter.6.cloned.1.call-start = ((), (), s32[]{:S(2)}) async-start(), calls=%async_computation.3 | async-start | bytes 2359296 | tf_op jit(solution)/shard_map/reduce_scatter | solution.py:65
  7.2 3.1 %copy-start.6 = (s32[8]{0:T(128)S(1)}, s32[8]{0:T(128)}, u32[]{:S(2)}) copy-start(s32[8]{0:T(128)} %param.14) | copy-start | bytes 100
  7.2 6.9 %copy-start.5 = (bf16[1,4,128,384]{3,2,1,0:T(8,128)(2,1)S(1)}, bf16[1,4,128,384]{3,2,1,0:T(8,128)(2,1)}, u32[]{:S(2)}) copy-start(bf16[1,4,128,384]{3,2,1,0:T(8,128)(2,1)} %param.8) | copy-start | bytes 1179652
  10.3 6.4 %copy-start.2 = (bf16[768,384]{1,0:T(8,128)(2,1)S(1)}, bf16[768,384]{1,0:T(8,128)(2,1)}, u32[]{:S(2)}) copy-start(bf16[768,384]{1,0:T(8,128)(2,1)} %param.11) | copy-start | bytes 1769476
  10.3 149.4 %all-reduce.3.cloned.1.call-start = ((), (), s32[]{:S(2)}) async-start(), calls=%async_computation.6 | async-start | bytes 6291456 | tf_op jit(solution)/shard_map/psum | solution.py:15
  16.6 1.8 copy-start.1
  18.4 2.8 %copy-start.7 = (s32[4]{0:T(128)S(1)}, s32[4]{0:T(128)}, u32[]{:S(2)}) copy-start(s32[4]{0:T(128)} %param.15) | copy-start | bytes 52
  27.6 159.4 %reduce-scatter.8.cloned.1.call-start = ((), (), s32[]{:S(2)}) async-start(), calls=%async_computation.4 | async-start | bytes 2359296 | tf_op jit(solution)/shard_map/reduce_scatter | solution.py:98
  174.5 1.1 copy-start.4
  177.4 82.3 %reduce-scatter.10.cloned.1.call-start = ((), (), s32[]{:S(2)}) async-start(), calls=%async_computation.5 | async-start | bytes 2654208
  183.0 2.8 %copy-start.3 = (bf16[768,384]{1,0:T(8,128)(2,1)S(1)}, bf16[768,384]{1,0:T(8,128)(2,1)}, u32[]{:S(2)}) copy-start(bf16[768,384]{1,0:T(8,128)(2,1)} %param.13) | copy-start | bytes 1769476
Sparse Core Ops, SparseCore 0:
  10.4 11.7 reduce-scatter.5
  27.8 131.9 all-reduce.2
  177.5 7.8 reduce-scatter.7
  189.1 70.5 reduce-scatter.9
where the time goes:
time: 269 us; the launch traced here: 268 us
  waiting for transfers between devices  202 us (75%)
  matrix products  26.4 us (10%)
  between operations  17.4 us (6%)
  other arithmetic  9.2 us (3%)
  local copies, waits for them, and re-layouts  8.19 us (3%)
  blocking collectives  4.81 us (2%)
    psum x1, waiting for transfers between devices, tied_total(): table = lax.psum(slots, ('seq', 'fam'))  131 us
    unnamed x5, waiting for transfers between devices  70.8 us
  transfers between devices with their start and end apart: 4, of which 2 were waited for; matrix products, arithmetic and copies ran while one was open for 6% of the time, Pallas kernels for 0%

commit v1 on v0

v1 whole, which is shorter than its diff:
```python
import functools

import jax
import jax.numpy as jnp
from jax import lax
from jax.experimental import pallas as pl
from jax.experimental.pallas import tpu as pltpu
from jax.sharding import PartitionSpec as P

D = 768
H = 12
MESH = pl.DeviceIdType.MESH
F32 = jnp.float32
BF16 = jnp.bfloat16


def dot(a, b, ca=1, cb=0):
    return lax.dot_general(a, b, (((ca,), (cb,)), ((), ())), preferred_element_type=F32)


def kernel(cfg, fam_ref, depth_ref, x_ref, cot_ref, wq_ref, wk_ref, wv_ref, wo_ref,
           out_ref, ig_ref, wg_ref,
           xf, cf, wor, mf, igr, igs, qs, ks, vs, os_, kp, vp, gqk, gv,
           part, xrecv, lrecv, rrecv, fsend, bsend, tsend, tfull, gpart, gxrecv, gfrecv, gbrecv, gfsend, gbsend,
           h_send, h_recv, x_send, x_recv, f_send, f_recv, b_send, b_recv, t_send, t_recv,
           gx_send, gx_recv, gf_send, gf_recv, gb_send, gb_recv):
    n_seq, n_fam, rows, cols, own_rows, fused = cfg
    width = x_ref.shape[1]
    n_pairs = width // 128
    head_size = D // H
    chunk = 256 // n_fam
    n_blocks = n_seq * n_fam
    steps = 2 * n_pairs
    z = lax.axis_index("seq")
    x = lax.axis_index("fam")
    h = lax.axis_index("head")
    other = 1 - h
    last = n_seq - 1

    def fam_at(d):
        return lax.rem(x + d + n_fam, n_fam)

    barrier = pltpu.get_barrier_semaphore()
    pl.semaphore_signal(barrier, inc=1, device_id={"head": other}, device_id_type=MESH)
    for d in range(1, n_fam):
        pl.semaphore_signal(barrier, inc=1, device_id={"fam": fam_at(d)}, device_id_type=MESH)

    @pl.when(z > 0)
    def _():
        pl.semaphore_signal(barrier, inc=1, device_id={"seq": z - 1}, device_id_type=MESH)

    @pl.when(z < last)
    def _():
        pl.semaphore_signal(barrier, inc=1, device_id={"seq": z + 1}, device_id_type=MESH)

    @pl.when(z == 0)
    def _():
        lrecv[...] = jnp.zeros_like(lrecv)
        if fused:
            gfrecv[...] = jnp.zeros_like(gfrecv)

    @pl.when(z == last)
    def _():
        rrecv[...] = jnp.zeros_like(rrecv)
        if fused:
            gbrecv[...] = jnp.zeros_like(gbrecv)

    pl.semaphore_wait(barrier, n_fam + jnp.where(z > 0, 1, 0) + jnp.where(z < last, 1, 0))

    mine = pl.ds(pl.multiple_of(h * width, 128), width)
    theirs = pl.ds(pl.multiple_of(other * width, 128), width)

    def to_head(src, dst, k):
        return pltpu.make_async_remote_copy(
            src_ref=src, dst_ref=dst, send_sem=h_send.at[k], recv_sem=h_recv.at[k],
            device_id={"head": other}, device_id_type=MESH)

    cx = to_head(x_ref, xf.at[:, mine], 0)
    cx.start()
    cc = to_head(cot_ref, cf.at[:, mine], 1)
    cc.start()
    cw = to_head(wo_ref.at[theirs, :], wor.at[:, mine], 2)
    cw.start()
    xf[:, mine] = x_ref[...]
    cf[:, mine] = cot_ref[...]
    wor[:, mine] = wo_ref[mine, :]

    base = z * n_fam

    def family(b):
        return fam_ref[b]

    def same(a, b):
        return jnp.where(a == b, 1.0, 0.0).astype(F32)

    f_rel = [family(base + fam_at(d)) for d in range(n_fam)]
    f_neg = [family(base + fam_at(-d)) for d in range(n_fam)]
    f_first = family(base)
    f_last = family(base + n_fam - 1)
    has_left = jnp.where(z > 0, 1.0, 0.0).astype(F32)
    has_right = jnp.where(z < last, 1.0, 0.0).astype(F32)
    f_prev = family(base - jnp.where(z > 0, 1, 0))
    f_next = family(base + n_fam - 1 + jnp.where(z < last, 1, 0))
    my_family = f_rel[0]
    first = lax.fori_loop(
        0, n_blocks, lambda b, c: c + jnp.where(fam_ref[b] < my_family, 1, 0), jnp.int32(0))
    my_depth = depth_ref[my_family]
    rank = base + x - first
    live = [jnp.where(rank * rows + r < my_depth, 1.0, 0.0).astype(F32) for r in range(rows)]
    scale = []
    for d in range(n_fam):
        deep = jnp.full((8, 128), depth_ref[f_rel[d]].astype(F32), F32)
        scale.append((1.0 / (jnp.sqrt(jnp.full((8, 128), float(head_size), F32)) * jnp.sqrt(deep)))[0:1])

    low = lax.broadcasted_iota(jnp.int32, (cols, 128), 1) < head_size

    def keep(value, stack, plain, masked):
        for r in range(rows):
            for p in range(n_pairs):
                v = value[r * cols:(r + 1) * cols, p * 128:(p + 1) * 128]
                v = v.astype(BF16).astype(F32)
                if masked:
                    v = v * live[r]
                lanes = slice(r * 128, (r + 1) * 128)
                stack[p, 0:cols, lanes] = jnp.where(low, v, 0.0).astype(BF16)
                stack[p, cols:2 * cols, lanes] = jnp.where(low, 0.0, v).astype(BF16)
                if plain is not None:
                    plain[p, :, lanes] = v.astype(BF16)

    def x_copy(s, d):
        to = fam_at(d)
        return pltpu.make_async_remote_copy(
            src_ref=part.at[s, pl.ds(pl.multiple_of(to * chunk, 16), chunk)],
            dst_ref=xrecv.at[s, d], send_sem=x_send.at[s, d], recv_sem=x_recv.at[s, d],
            device_id={"fam": to}, device_id_type=MESH)

    cx.wait()
    keep(dot(xf[...], wq_ref[...]), qs, None, True)
    keep(dot(xf[...], wk_ref[...]), ks, kp, True)
    for p in range(n_pairs):
        part[p] = dot(qs[p], kp[p], 1, 1)
        for d in range(1, n_fam):
            x_copy(p, d).start()
    keep(dot(xf[...], wv_ref[...]), vs, vp, False)
    cc.wait()
    cw.wait()
    keep(dot(cf[...], wor[...], 1, 1), os_, None, False)
    for p in range(n_pairs):
        part[n_pairs + p] = dot(os_[p], vp[p], 1, 1)
        for d in range(1, n_fam):
            x_copy(n_pairs + p, d).start()

    own = pl.ds(pl.multiple_of(x * chunk, 16), chunk)

    def f_copy(s):
        return pltpu.make_async_remote_copy(
            src_ref=fsend.at[s], dst_ref=lrecv.at[s], send_sem=f_send.at[s], recv_sem=f_recv.at[s],
            device_id={"seq": z + 1}, device_id_type=MESH)

    def b_copy(s):
        return pltpu.make_async_remote_copy(
            src_ref=bsend.at[s], dst_ref=rrecv.at[s], send_sem=b_send.at[s], recv_sem=b_recv.at[s],
            device_id={"seq": z - 1}, device_id_type=MESH)

    def row_terms(s):
        return [part[s, own]] + [xrecv[s, d] for d in range(1, n_fam)]

    def chain(t, carry):
        sf = t - z
        sb = t - (last - z)

        @pl.when((sf >= 0) & (sf < steps))
        def _():
            @pl.when(z <= last - z)
            def _():
                for d in range(1, n_fam):
                    x_copy(sf, d).wait_recv()

            @pl.when(z > 0)
            def _():
                f_copy(sf).wait_recv()

            @pl.when(z < last)
            def _():
                total = (has_left * same(f_prev, f_last)) * lrecv[sf]
                for d, term in enumerate(row_terms(sf)):
                    total = total + same(f_neg[d], f_last) * term
                fsend[sf] = total
                f_copy(sf).start()

        @pl.when((sb >= 0) & (sb < steps))
        def _():
            @pl.when(z > last - z)
            def _():
                for d in range(1, n_fam):
                    x_copy(sb, d).wait_recv()

            @pl.when(z < last)
            def _():
                b_copy(sb).wait_recv()

            @pl.when(z > 0)
            def _():
                total = (has_right * same(f_next, f_first)) * rrecv[sb]
                for d, term in enumerate(row_terms(sb)):
                    total = total + same(f_neg[d], f_first) * term
                bsend[sb] = total
                b_copy(sb).start()

        return carry

    lax.fori_loop(0, steps + last, chain, jnp.int32(0))

    def t_copy(k, p, d):
        return pltpu.make_async_remote_copy(
            src_ref=tsend.at[k, p, d], dst_ref=tfull.at[k, p, own],
            send_sem=t_send.at[k, p, d], recv_sem=t_recv.at[k, p, d],
            device_id={"fam": fam_at(d)}, device_id_type=MESH)

    def t_wait(k, p, d):
        came = pl.ds(pl.multiple_of(fam_at(-d) * chunk, 16), chunk)
        pltpu.make_async_remote_copy(
            src_ref=tsend.at[k, p, d], dst_ref=tfull.at[k, p, came],
            send_sem=t_send.at[k, p, d], recv_sem=t_recv.at[k, p, d],
            device_id={"fam": fam_at(d)}, device_id_type=MESH).wait_recv()

    for p in range(n_pairs):
        sums = []
        for s in (p, n_pairs + p):
            terms = row_terms(s)
            left, right = lrecv[s], rrecv[s]
            for e in range(n_fam):
                total = (has_left * same(f_prev, f_rel[e])) * left
                total = total + (has_right * same(f_next, f_rel[e])) * right
                for d in range(n_fam):
                    total = total + same(f_neg[d], f_rel[e]) * terms[d]
                sums.append(total)
        for e in list(range(1, n_fam)) + [0]:
            expo = jnp.exp(sums[e] * scale[e])
            attention = expo / jnp.sum(expo, axis=-1, keepdims=True)
            grad = sums[n_fam + e]
            centred = grad - jnp.sum(attention * grad, axis=-1, keepdims=True)
            pair = (attention.astype(BF16), (scale[e] * attention * centred).astype(BF16))
            for k in (1, 0):
                if e == 0:
                    tfull[k, p, own] = pair[k]
                else:
                    tsend[k, p, e] = pair[k]
                    t_copy(k, p, e).start()

    def both(k, p):
        return jnp.concatenate([tfull[k, p, 0:cols], tfull[k, p, cols:2 * cols]], axis=1)

    def spread(value, ref, at):
        for r in range(rows):
            ref[r * cols:(r + 1) * cols, at:at + 128] = value[:, r * 128:(r + 1) * 128].astype(BF16)

    for p in range(n_pairs):
        for d in range(1, n_fam):
            t_wait(1, p, d)
        spread(dot(both(1, p), ks[p]), gqk, p * 128)
        spread(dot(tfull[1, p], qs[p], 0, 0), gqk, width + p * 128)

    for c in range(D // 256):
        piece = dot(xf[:, c * 256:(c + 1) * 256], gqk[...], 0, 0)
        if fused:
            gpart[c * 256:(c + 1) * 256] = piece.astype(BF16)
        else:
            wg_ref[c * 256:(c + 1) * 256] = piece

    def part_rows(to_z, to_x):
        return pl.ds(pl.multiple_of((to_z * n_fam + to_x) * own_rows, 16), own_rows)

    def gx_copy(to_z, d):
        return pltpu.make_async_remote_copy(
            src_ref=gpart.at[part_rows(to_z, fam_at(d))], dst_ref=gxrecv.at[to_z, d],
            send_sem=gx_send.at[to_z, d], recv_sem=gx_recv.at[to_z, d],
            device_id={"fam": fam_at(d)}, device_id_type=MESH)

    order = []
    for k in range(n_seq):
        order += [k // 2 if k % 2 == 0 else n_seq - 1 - k // 2]
    if fused:
        for to_z in order:
            for d in range(1, n_fam):
                gx_copy(to_z, d).start()

    for p in range(n_pairs):
        for d in range(1, n_fam):
            t_wait(0, p, d)
        mixed = dot(both(0, p), vs[p])
        for r in range(rows):
            mf[r * cols:(r + 1) * cols, pl.ds(pl.multiple_of(h * width + p * 128, 128), 128)] = (
                mixed[:, r * 128:(r + 1) * 128].astype(BF16))
    cm = to_head(mf.at[:, mine], mf.at[:, mine], 3)
    cm.start()
    for p in range(n_pairs):
        spread(dot(tfull[0, p], os_[p], 0, 0), gv, p * 128)

    def back(at):
        return (dot(gqk[:, 0:width], wq_ref[at, :], 1, 1)
                + dot(gqk[:, width:2 * width], wk_ref[at, :], 1, 1)
                + dot(gv[...], wv_ref[at, :], 1, 1))

    igs[...] = back(theirs).astype(igs.dtype)
    ci = to_head(igs, igr, 4)
    ci.start()
    cm.wait()
    out_ref[...] = dot(mf[...], wo_ref[...]).astype(BF16)
    mine_grad = back(mine)
    ci.wait()
    ig_ref[...] = (mine_grad + igr[...].astype(F32)).astype(BF16)

    if fused:
        for to_z in order:
            for d in range(1, n_fam):
                gx_copy(to_z, d).wait_recv()

        def g_term(to_z):
            total = gpart[part_rows(to_z, x)].astype(F32)
            for d in range(1, n_fam):
                total = total + gxrecv[to_z, d].astype(F32)
            return total

        def gf_copy(to_z):
            return pltpu.make_async_remote_copy(
                src_ref=gfsend.at[to_z], dst_ref=gfrecv.at[to_z],
                send_sem=gf_send.at[to_z], recv_sem=gf_recv.at[to_z],
                device_id={"seq": z + 1}, device_id_type=MESH)

        def gb_copy(to_z):
            return pltpu.make_async_remote_copy(
                src_ref=gbsend.at[to_z], dst_ref=gbrecv.at[to_z],
                send_sem=gb_send.at[to_z], recv_sem=gb_recv.at[to_z],
                device_id={"seq": z - 1}, device_id_type=MESH)

        def g_chain(t, carry):
            @pl.when(t >= z)
            def _():
                to_z = last - (t - z)

                @pl.when(z > 0)
                def _():
                    gf_copy(to_z).wait_recv()

                gfsend[to_z] = (g_term(to_z) + gfrecv[to_z].astype(F32)).astype(BF16)
                gf_copy(to_z).start()

            @pl.when(t >= last - z)
            def _():
                to_z = t - (last - z)

                @pl.when(z < last)
                def _():
                    gb_copy(to_z).wait_recv()

                gbsend[to_z] = (g_term(to_z) + gbrecv[to_z].astype(F32)).astype(BF16)
                gb_copy(to_z).start()

            return carry

        lax.fori_loop(0, last, g_chain, jnp.int32(0))

        @pl.when(z > 0)
        def _():
            gf_copy(z).wait_recv()

        @pl.when(z < last)
        def _():
            gb_copy(z).wait_recv()

        wg_ref[...] = g_term(z) + gfrecv[z].astype(F32) + gbrecv[z].astype(F32)

        def g_sent(t, carry):
            @pl.when(t >= z)
            def _():
                gf_copy(last - (t - z)).wait_send()

            @pl.when(t >= last - z)
            def _():
                gb_copy(t - (last - z)).wait_send()

            return carry

        lax.fori_loop(0, last, g_sent, jnp.int32(0))
        for to_z in order:
            for d in range(1, n_fam):
                gx_copy(to_z, d).wait_send()

    for s in range(steps):
        for d in range(1, n_fam):
            x_copy(s, d).wait_send()

        @pl.when(z < last)
        def _():
            f_copy(s).wait_send()

        @pl.when(z > 0)
        def _():
            b_copy(s).wait_send()
    for k in range(2):
        for p in range(n_pairs):
            for d in range(1, n_fam):
                t_copy(k, p, d).wait_send()


def shards(cfg, blocks, cotangent, w_query, w_key, w_value, w_out, block_family, family_depth):
    n_seq, n_fam, rows, cols, own_rows, fused = cfg
    tokens = rows * cols
    width = blocks.shape[3]
    n_pairs = width // 128
    steps = 2 * n_pairs
    chunk = 256 // n_fam
    lanes = rows * 128
    vmem = pltpu.VMEM
    dma = pltpu.SemaphoreType.DMA
    g_z, g_r = (n_seq, own_rows) if fused else (1, 16)
    g_all = D if fused else 16
    scratch = [
        vmem((tokens, D), BF16), vmem((tokens, D), BF16), vmem((width, D), BF16),
        vmem((tokens, D), BF16), vmem((tokens, width), BF16), vmem((tokens, width), BF16),
        vmem((n_pairs, 256, lanes), BF16), vmem((n_pairs, 256, lanes), BF16),
        vmem((n_pairs, 256, lanes), BF16), vmem((n_pairs, 256, lanes), BF16),
        vmem((n_pairs, 128, lanes), BF16), vmem((n_pairs, 128, lanes), BF16),
        vmem((tokens, 2 * width), BF16), vmem((tokens, width), BF16),
        vmem((steps, 256, 128), F32), vmem((steps, n_fam, chunk, 128), F32),
        vmem((steps, chunk, 128), F32), vmem((steps, chunk, 128), F32),
        vmem((steps, chunk, 128), F32), vmem((steps, chunk, 128), F32),
        vmem((2, n_pairs, n_fam, chunk, 128), BF16), vmem((2, n_pairs, 256, 128), BF16),
        vmem((g_all, 2 * width), BF16), vmem((g_z, n_fam, g_r, 2 * width), BF16),
        vmem((g_z, g_r, 2 * width), BF16), vmem((g_z, g_r, 2 * width), BF16),
        vmem((g_z, g_r, 2 * width), BF16), vmem((g_z, g_r, 2 * width), BF16),
        dma((5,)), dma((5,)), dma((steps, n_fam)), dma((steps, n_fam)),
        dma((steps,)), dma((steps,)), dma((steps,)), dma((steps,)),
        dma((2, n_pairs, n_fam)), dma((2, n_pairs, n_fam)),
        dma((g_z, n_fam)), dma((g_z, n_fam)), dma((g_z,)), dma((g_z,)), dma((g_z,)), dma((g_z,)),
    ]
    spec = pl.BlockSpec(memory_space=pltpu.VMEM)
    smem = pl.BlockSpec(memory_space=pltpu.SMEM)
    layer_out, input_grad, weight_grad = pl.pallas_call(
        functools.partial(kernel, cfg),
        out_shape=(
            jax.ShapeDtypeStruct((tokens, width), BF16),
            jax.ShapeDtypeStruct((tokens, width), BF16),
            jax.ShapeDtypeStruct((own_rows if fused else D, 2 * width), F32),
        ),
        in_specs=[smem, smem] + [spec] * 6,
        out_specs=(spec, spec, spec),
        scratch_shapes=scratch,
        compiler_params=pltpu.CompilerParams(
            collective_id=0, has_side_effects=True, vmem_limit_bytes=56 * 1024 * 1024),
    )(block_family, family_depth, blocks.reshape(tokens, width), cotangent.reshape(tokens, width),
      w_query, w_key, w_value, w_out)
    if not fused:
        weight_grad = lax.psum_scatter(weight_grad, ("seq", "fam"), scatter_dimension=0, tiled=True)
    return (
        layer_out.reshape(blocks.shape),
        input_grad.reshape(blocks.shape),
        weight_grad.reshape(own_rows, 2, width),
    )


def solution(mesh):
    n_seq, n_fam = mesh.shape["seq"], mesh.shape["fam"]

    def local(*arrays):
        own_rows = D // (n_seq * n_fam)
        blocks = arrays[0]
        rows = blocks.shape[0] * blocks.shape[1]
        cfg = (n_seq, n_fam, rows, blocks.shape[2], own_rows, own_rows % 16 == 0)
        return shards(cfg, *arrays)

    token_spec = P(("groups", "seq", "fam"), None, None, "head")
    weight_spec = P(None, "head")
    return jax.shard_map(
        local,
        mesh=mesh,
        in_specs=(token_spec, token_spec, weight_spec, weight_spec, weight_spec, weight_spec,
                  P("groups"), P("groups")),
        out_specs=(token_spec, token_spec, P(("groups", "seq", "fam"), None, "head")),
        check_vma=False,
    )
```

time: 269 us -> 71.7 us (0.27)
  waiting for transfers between devices: 202 us -> 0 us
  Pallas kernels: 0 us -> 67.1 us
  matrix products: 26.4 us -> 0 us
  between operations: 17.4 us -> 0.65 us
  other arithmetic: 9.2 us -> 0 us
  blocking collectives: 4.81 us -> 0 us
  local copies, waits for them, and re-layouts: 8.19 us -> 3.77 us
    psum x1 -> x0, waiting for transfers between devices: 131 us -> none  [tied_total(): table = lax.psum(slots, ('seq', 'fam'))]
    unnamed x5 -> x0, waiting for transfers between devices: 70.8 us -> none
    pallas_call x0 -> x1, Pallas kernels: none -> 67.1 us  [shards(): pl.pallas_call(functools.partial(kernel, cfg), out_shape=(jax.ShapeDtypeS...]
    dot_general x15 -> x0, matrix products: 26.4 us -> none  [the longest x1 5.37 us: shards(): jnp.einsum('hij,rihd->rjhd', logit_grad, query_rows, preferred_element_ty...]
    all_gather x2 -> x0, blocking collectives: 4.81 us -> none  [the longest x1 2.45 us: shards(): full_blocks = lax.all_gather(blocks, 'head', axis=3, tiled=True)]
    convert_element_type x4 -> x0, other arithmetic: 4.4 us -> none  [the longest x1 1.92 us: shards(): input_grad = lax.psum_scatter(grad_terms, 'head', scatter_dimension=1, ti...]
  transfers between devices with their start and end apart: 4 -> 0, of which waited for: 2 -> 0; matrix products, arithmetic and copies ran while one was open for 6% -> 0% of each run, Pallas kernels for 0% -> 0%
where the time goes in v1:
time: 71.7 us; the launch traced here: 71.5 us
  Pallas kernels  67.1 us (94%)
  local copies, waits for them, and re-layouts  3.77 us (5%)
    pallas_call x1, Pallas kernels, shards(): pl.pallas_call(functools.partial(kernel, cfg), out_shape=(jax.ShapeDtypeS...  67.1 us
    unnamed x6, local copies, waits for them, and re-layouts  1.89 us
    reshape x1, local copies, waits for them, and re-layouts, shards(): weight_grad.reshape(own_rows, 2, width)  1.88 us

profile of v1, /device:TPU:0, one launch (start us, length us, event | category | flops | bytes accessed | tf_op | source)
XLA Modules:
  0.0 71.5 jit_solution(16419611949032233479)
XLA Ops:
  0.6 67.1 %shard_map.103 = (bf16[512,384]{1,0:T(8,128)(2,1)}, bf16[512,384]{1,0:T(8,128)(2,1)}, f32[96,768]{1,0:T(8,128)}) custom-call(s32[8]{0:T(128)} %fam_ref.1, s32[4]{0:T(128)} %depth_ref.1, bf16[512,384]{1,0:T(8,128)(2,1)} %bitcast.6, bf16[512,384]{1,0:T(8,128)(2,1)} %bitcast.7, bf16[768,384]{1,0:T(8,128)(2,1)} %wq_ref.1, bf16[768,384]{1,0:T(8,128)(2,1)} %wk_ref.1, ...), custom_call_target="tpu_custom_call" | custom-call | tf_op jit(solution)/shard_map/pallas_call | solution.py:440
  67.7 0.0 copy-start.1
  67.7 1.9 %reshape.25 = f32[96,2,384]{2,1,0:T(2,128)} reshape(f32[96,768]{1,0:T(8,128)} %get-tuple-element.8) | data formatting | bytes 589824 | tf_op jit(solution)/shard_map/reshape | solution.py:459
  69.6 0.0 copy-done.1
  69.6 0.0 copy-start
  69.6 0.7 %copy.13 = bf16[1,4,128,384]{3,2,1,0:T(8,128)(2,1)} copy(bf16[1,4,128,384]{3,2,1,0:T(8,128)(2,1)S(1)} %bitcast.5) | data formatting | bytes 786432
  70.4 0.4 copy-done
  70.8 0.7 %copy.14 = bf16[1,4,128,384]{3,2,1,0:T(8,128)(2,1)} copy(bf16[1,4,128,384]{3,2,1,0:T(8,128)(2,1)S(1)} %bitcast.4) | data formatting | bytes 786432
Async XLA Ops:
  67.7 1.9 %copy-start.1 = (bf16[512,384]{1,0:T(8,128)(2,1)S(1)}, bf16[512,384]{1,0:T(8,128)(2,1)}, u32[]{:S(2)}) copy-start(bf16[512,384]{1,0:T(8,128)(2,1)} %get-tuple-element.6) | copy-start | bytes 1179652
  69.6 1.1 %copy-start = (bf16[512,384]{1,0:T(8,128)(2,1)S(1)}, bf16[512,384]{1,0:T(8,128)(2,1)}, u32[]{:S(2)}) copy-start(bf16[512,384]{1,0:T(8,128)(2,1)} %get-tuple-element.7) | copy-start | bytes 1179652

commit v2 on v1

--- a/solution.py
+++ b/solution.py
@@ -21,9 +21,11 @@
 def kernel(cfg, fam_ref, depth_ref, x_ref, cot_ref, wq_ref, wk_ref, wv_ref, wo_ref,
            out_ref, ig_ref, wg_ref,
            xf, cf, wor, mf, igr, igs, qs, ks, vs, os_, kp, vp, gqk, gv,
-           part, xrecv, lrecv, rrecv, fsend, bsend, tsend, tfull, gpart, gxrecv, gfrecv, gbrecv, gfsend, gbsend,
+           part, xrecv, lrecv, rrecv, fsend, bsend, tsend, tfull, gpart, gxrecv,
+           qfrecv, qbrecv, qfsend, qbsend, kfrecv, kbrecv, kfsend, kbsend, kxsend, kxrecv,
            h_send, h_recv, x_send, x_recv, f_send, f_recv, b_send, b_recv, t_send, t_recv,
-           gx_send, gx_recv, gf_send, gf_recv, gb_send, gb_recv):
+           gx_send, gx_recv, qf_send, qf_recv, qb_send, qb_recv,
+           kf_send, kf_recv, kb_send, kb_recv, kx_send, kx_recv):
     n_seq, n_fam, rows, cols, own_rows, fused = cfg
     width = x_ref.shape[1]
     n_pairs = width // 128
@@ -57,13 +59,15 @@
     def _():
         lrecv[...] = jnp.zeros_like(lrecv)
         if fused:
-            gfrecv[...] = jnp.zeros_like(gfrecv)
+            qfrecv[...] = jnp.zeros_like(qfrecv)
+            kfrecv[...] = jnp.zeros_like(kfrecv)
 
     @pl.when(z == last)
     def _():
         rrecv[...] = jnp.zeros_like(rrecv)
         if fused:
-            gbrecv[...] = jnp.zeros_like(gbrecv)
+            qbrecv[...] = jnp.zeros_like(qbrecv)
+            kbrecv[...] = jnp.zeros_like(kbrecv)
 
     pl.semaphore_wait(barrier, n_fam + jnp.where(z > 0, 1, 0) + jnp.where(z < last, 1, 0))
 
@@ -255,28 +259,118 @@
         for r in range(rows):
             ref[r * cols:(r + 1) * cols, at:at + 128] = value[:, r * 128:(r + 1) * 128].astype(BF16)
 
-    for p in range(n_pairs):
-        for d in range(1, n_fam):
-            t_wait(1, p, d)
-        spread(dot(both(1, p), ks[p]), gqk, p * 128)
-        spread(dot(tfull[1, p], qs[p], 0, 0), gqk, width + p * 128)
-
-    for c in range(D // 256):
-        piece = dot(xf[:, c * 256:(c + 1) * 256], gqk[...], 0, 0)
-        if fused:
-            gpart[c * 256:(c + 1) * 256] = piece.astype(BF16)
-        else:
-            wg_ref[c * 256:(c + 1) * 256] = piece
-
-    def part_rows(to_z, to_x):
-        return pl.ds(pl.multiple_of((to_z * n_fam + to_x) * own_rows, 16), own_rows)
+    def part_rows(to_z, to_x, count):
+        return pl.ds(pl.multiple_of((to_z * n_fam + to_x) * own_rows, 16), count)
 
     def gx_copy(to_z, d):
         return pltpu.make_async_remote_copy(
-            src_ref=gpart.at[part_rows(to_z, fam_at(d))], dst_ref=gxrecv.at[to_z, d],
+            src_ref=gpart.at[0, part_rows(to_z, fam_at(d), own_rows)], dst_ref=gxrecv.at[to_z, d],
             send_sem=gx_send.at[to_z, d], recv_sem=gx_recv.at[to_z, d],
             device_id={"fam": fam_at(d)}, device_id_type=MESH)
 
+    def kx_copy(d):
+        return pltpu.make_async_remote_copy(
+            src_ref=kxsend.at[fam_at(d)], dst_ref=kxrecv.at[d], send_sem=kx_send.at[d], recv_sem=kx_recv.at[d],
+            device_id={"fam": fam_at(d)}, device_id_type=MESH)
+
+    def q_term(to_z):
+        total = gpart[0, part_rows(to_z, x, own_rows)].astype(F32)
+        for d in range(1, n_fam):
+            gx_copy(to_z, d).wait_recv()
+            total = total + gxrecv[to_z, d].astype(F32)
+        return total
+
+    def k_term(to_z):
+        return gpart[1, part_rows(to_z, 0, n_fam * own_rows)].astype(F32)
+
+    def two_way(term, fsrc, fdst, fs, fr, bsrc, bdst, bs, br):
+        def fcopy(to_z):
+            return pltpu.make_async_remote_copy(
+                src_ref=fsrc.at[to_z], dst_ref=fdst.at[to_z], send_sem=fs.at[to_z], recv_sem=fr.at[to_z],
+                device_id={"seq": z + 1}, device_id_type=MESH)
+
+        def bcopy(to_z):
+            return pltpu.make_async_remote_copy(
+                src_ref=bsrc.at[to_z], dst_ref=bdst.at[to_z], send_sem=bs.at[to_z], recv_sem=br.at[to_z],
+                device_id={"seq": z - 1}, device_id_type=MESH)
+
+        def step(t):
+            @pl.when(t >= z)
+            def _():
+                to_z = last - (t - z)
+                total = term(to_z)
+
+                @pl.when(z > 0)
+                def _():
+                    fcopy(to_z).wait_recv()
+
+                fsrc[to_z] = (total + fdst[to_z].astype(F32)).astype(BF16)
+                fcopy(to_z).start()
+
+            @pl.when(t >= last - z)
+            def _():
+                to_z = t - (last - z)
+                total = term(to_z)
+
+                @pl.when(z < last)
+                def _():
+                    bcopy(to_z).wait_recv()
+
+                bsrc[to_z] = (total + bdst[to_z].astype(F32)).astype(BF16)
+                bcopy(to_z).start()
+
+        def finish():
+            total = term(z)
+
+            @pl.when(z > 0)
+            def _():
+                fcopy(z).wait_recv()
+
+            @pl.when(z < last)
+            def _():
+                bcopy(z).wait_recv()
+
+            return total + fdst[z].astype(F32) + bdst[z].astype(F32)
+
+        def sent():
+            for t in range(last):
+                @pl.when(t >= z)
+                def _():
+                    fcopy(last - (t - z)).wait_send()
+
+                @pl.when(t >= last - z)
+                def _():
+                    bcopy(t - (last - z)).wait_send()
+
+        def steps_of(lo, hi):
+            if fused:
+                for t in range(lo, min(hi, last)):
+                    step(t)
+
+        return steps_of, finish, sent
+
+    q_steps, q_finish, q_sent = two_way(
+        q_term, qfsend, qfrecv, qf_send, qf_recv, qbsend, qbrecv, qb_send, qb_recv)
+    k_steps, k_finish, k_sent = two_way(
+        k_term, kfsend, kfrecv, kf_send, kf_recv, kbsend, kbrecv, kb_send, kb_recv)
+
+    def weight_part(k):
+        for c in range(D // 256):
+            piece = dot(xf[:, c * 256:(c + 1) * 256], gqk[:, k * width:(k + 1) * width], 0, 0)
+            if fused:
+                gpart[k, c * 256:(c + 1) * 256] = piece.astype(BF16)
+            else:
+                wg_ref[c * 256:(c + 1) * 256, k * width:(k + 1) * width] = piece
+
+    for p in range(n_pairs):
+        for d in range(1, n_fam):
+            t_wait(1, p, d)
+        spread(dot(tfull[1, p], qs[p], 0, 0), gqk, width + p * 128)
+    weight_part(1)
+    k_steps(0, 1)
+    for p in range(n_pairs):
+        spread(dot(both(1, p), ks[p]), gqk, p * 128)
+    weight_part(0)
     order = []
     for k in range(n_seq):
         order += [k // 2 if k % 2 == 0 else n_seq - 1 - k // 2]
@@ -294,6 +388,7 @@
                 mixed[:, r * 128:(r + 1) * 128].astype(BF16))
     cm = to_head(mf.at[:, mine], mf.at[:, mine], 3)
     cm.start()
+    k_steps(1, 2)
     for p in range(n_pairs):
         spread(dot(tfull[0, p], os_[p], 0, 0), gv, p * 128)
 
@@ -302,87 +397,34 @@
                 + dot(gqk[:, width:2 * width], wk_ref[at, :], 1, 1)
                 + dot(gv[...], wv_ref[at, :], 1, 1))
 
+    q_steps(0, 1)
     igs[...] = back(theirs).astype(igs.dtype)
     ci = to_head(igs, igr, 4)
     ci.start()
+    k_steps(2, last)
+    q_steps(1, 2)
+    if fused:
+        summed = k_finish()
+        kxsend[...] = summed.astype(BF16).reshape(n_fam, own_rows, width)
+        for d in range(1, n_fam):
+            kx_copy(d).start()
     cm.wait()
     out_ref[...] = dot(mf[...], wo_ref[...]).astype(BF16)
+    q_steps(2, last)
     mine_grad = back(mine)
     ci.wait()
     ig_ref[...] = (mine_grad + igr[...].astype(F32)).astype(BF16)
-
     if fused:
-        for to_z in order:
-            for d in range(1, n_fam):
-                gx_copy(to_z, d).wait_recv()
-
-        def g_term(to_z):
-            total = gpart[part_rows(to_z, x)].astype(F32)
-            for d in range(1, n_fam):
-                total = total + gxrecv[to_z, d].astype(F32)
-            return total
-
-        def gf_copy(to_z):
-            return pltpu.make_async_remote_copy(
-                src_ref=gfsend.at[to_z], dst_ref=gfrecv.at[to_z],
-                send_sem=gf_send.at[to_z], recv_sem=gf_recv.at[to_z],
-                device_id={"seq": z + 1}, device_id_type=MESH)
-
-        def gb_copy(to_z):
-            return pltpu.make_async_remote_copy(
-                src_ref=gbsend.at[to_z], dst_ref=gbrecv.at[to_z],
-                send_sem=gb_send.at[to_z], recv_sem=gb_recv.at[to_z],
-                device_id={"seq": z - 1}, device_id_type=MESH)
-
-        def g_chain(t, carry):
-            @pl.when(t >= z)
-            def _():
-                to_z = last - (t - z)
-
-                @pl.when(z > 0)
-                def _():
-                    gf_copy(to_z).wait_recv()
-
-                gfsend[to_z] = (g_term(to_z) + gfrecv[to_z].astype(F32)).astype(BF16)
-                gf_copy(to_z).start()
-
-            @pl.when(t >= last - z)
-            def _():
-                to_z = t - (last - z)
-
-                @pl.when(z < last)
-                def _():
-                    gb_copy(to_z).wait_recv()
-
-                gbsend[to_z] = (g_term(to_z) + gbrecv[to_z].astype(F32)).astype(BF16)
-                gb_copy(to_z).start()
-
-            return carry
-
-        lax.fori_loop(0, last, g_chain, jnp.int32(0))
-
-        @pl.when(z > 0)
-        def _():
-            gf_copy(z).wait_recv()
-
-        @pl.when(z < last)
-        def _():
-            gb_copy(z).wait_recv()
-
-        wg_ref[...] = g_term(z) + gfrecv[z].astype(F32) + gbrecv[z].astype(F32)
-
-        def g_sent(t, carry):
-            @pl.when(t >= z)
-            def _():
-                gf_copy(last - (t - z)).wait_send()
-
-            @pl.when(t >= last - z)
-            def _():
-                gb_copy(t - (last - z)).wait_send()
-
-            return carry
-
-        lax.fori_loop(0, last, g_sent, jnp.int32(0))
+        wg_ref[:, 0, :] = q_finish()
+        total = kxsend[x].astype(F32)
+        for d in range(1, n_fam):
+            kx_copy(d).wait_recv()
+            total = total + kxrecv[d].astype(F32)
+        wg_ref[:, 1, :] = total
+        q_sent()
+        k_sent()
+        for d in range(1, n_fam):
+            kx_copy(d).wait_send()
         for to_z in order:
             for d in range(1, n_fam):
                 gx_copy(to_z, d).wait_send()
@@ -427,13 +469,17 @@
         vmem((steps, chunk, 128), F32), vmem((steps, chunk, 128), F32),
         vmem((steps, chunk, 128), F32), vmem((steps, chunk, 128), F32),
         vmem((2, n_pairs, n_fam, chunk, 128), BF16), vmem((2, n_pairs, 256, 128), BF16),
-        vmem((g_all, 2 * width), BF16), vmem((g_z, n_fam, g_r, 2 * width), BF16),
-        vmem((g_z, g_r, 2 * width), BF16), vmem((g_z, g_r, 2 * width), BF16),
-        vmem((g_z, g_r, 2 * width), BF16), vmem((g_z, g_r, 2 * width), BF16),
+        vmem((2, g_all, width), BF16), vmem((g_z, n_fam, g_r, width), BF16),
+        vmem((g_z, g_r, width), BF16), vmem((g_z, g_r, width), BF16),
+        vmem((g_z, g_r, width), BF16), vmem((g_z, g_r, width), BF16),
+        vmem((g_z, n_fam * g_r, width), BF16), vmem((g_z, n_fam * g_r, width), BF16),
+        vmem((g_z, n_fam * g_r, width), BF16), vmem((g_z, n_fam * g_r, width), BF16),
+        vmem((n_fam, g_r, width), BF16), vmem((n_fam, g_r, width), BF16),
         dma((5,)), dma((5,)), dma((steps, n_fam)), dma((steps, n_fam)),
         dma((steps,)), dma((steps,)), dma((steps,)), dma((steps,)),
         dma((2, n_pairs, n_fam)), dma((2, n_pairs, n_fam)),
         dma((g_z, n_fam)), dma((g_z, n_fam)), dma((g_z,)), dma((g_z,)), dma((g_z,)), dma((g_z,)),
+        dma((g_z,)), dma((g_z,)), dma((g_z,)), dma((g_z,)), dma((n_fam,)), dma((n_fam,)),
     ]
     spec = pl.BlockSpec(memory_space=pltpu.VMEM)
     smem = pl.BlockSpec(memory_space=pltpu.SMEM)
@@ -442,7 +488,7 @@
         out_shape=(
             jax.ShapeDtypeStruct((tokens, width), BF16),
             jax.ShapeDtypeStruct((tokens, width), BF16),
-            jax.ShapeDtypeStruct((own_rows if fused else D, 2 * width), F32),
+            jax.ShapeDtypeStruct((own_rows, 2, width) if fused else (D, 2 * width), F32),
         ),
         in_specs=[smem, smem] + [spec] * 6,
         out_specs=(spec, spec, spec),

time: 71.7 us -> 68 us (0.948)
  Pallas kernels: 67.1 us -> 63.5 us
    pallas_call x1, Pallas kernels: 67.1 us -> 63.5 us  [shards(): pl.pallas_call(functools.partial(kernel, cfg), out_shape=(jax.ShapeDtypeS...]
    reshape x1 -> x0, local copies, waits for them, and re-layouts: 1.88 us -> none  [shards(): weight_grad.reshape(own_rows, 2, width)]
    unnamed x6 -> x7, local copies, waits for them, and re-layouts: 1.89 us -> 3.65 us
where the time goes in v2:
time: 68 us; the launch traced here: 67.8 us
  Pallas kernels  63.5 us (93%)
  local copies, waits for them, and re-layouts  3.65 us (5%)
    pallas_call x1, Pallas kernels, shards(): pl.pallas_call(functools.partial(kernel, cfg), out_shape=(jax.ShapeDtypeS...  63.5 us
    unnamed x7, local copies, waits for them, and re-layouts  3.65 us

profile of v2, /device:TPU:0, one launch (start us, length us, event | category | flops | bytes accessed | tf_op | source)
XLA Modules:
  0.0 67.8 jit_solution(14582811567569441408)
XLA Ops:
  0.6 63.5 %shard_map.103 = (bf16[512,384]{1,0:T(8,128)(2,1)}, bf16[512,384]{1,0:T(8,128)(2,1)}, f32[96,2,384]{2,1,0:T(2,128)}) custom-call(s32[8]{0:T(128)} %fam_ref.1, s32[4]{0:T(128)} %depth_ref.1, bf16[512,384]{1,0:T(8,128)(2,1)} %bitcast.6, bf16[512,384]{1,0:T(8,128)(2,1)} %bitcast.7, bf16[768,384]{1,0:T(8,128)(2,1)} %wq_ref.1, bf16[768,384]{1,0:T(8,128)(2,1)} %wk_ref.1, ...), custom_call_target="tpu_custom_call" | custom-call | tf_op jit(solution)/shard_map/pallas_call | solution.py:486
  64.1 0.0 copy-start
  64.1 1.8 %copy.14 = bf16[1,4,128,384]{3,2,1,0:T(8,128)(2,1)} copy(bf16[1,4,128,384]{3,2,1,0:T(8,128)(2,1)} %bitcast.5) | data formatting | bytes 786432
  65.9 0.0 copy-done
  65.9 0.0 copy-start.1
  65.9 0.7 %copy.15 = bf16[1,4,128,384]{3,2,1,0:T(8,128)(2,1)} copy(bf16[1,4,128,384]{3,2,1,0:T(8,128)(2,1)S(1)} %bitcast.4) | data formatting | bytes 786432
  66.7 0.4 copy-done.1
  67.0 0.7 %copy.16 = f32[96,2,384]{2,1,0:T(2,128)} copy(f32[96,2,384]{2,1,0:T(2,128)S(1)} %copy-done.1) | data formatting | bytes 589824
Async XLA Ops:
  64.1 1.8 %copy-start = (bf16[512,384]{1,0:T(8,128)(2,1)S(1)}, bf16[512,384]{1,0:T(8,128)(2,1)}, u32[]{:S(2)}) copy-start(bf16[512,384]{1,0:T(8,128)(2,1)} %get-tuple-element.7) | copy-start | bytes 1179652
  65.9 1.1 %copy-start.1 = (f32[96,2,384]{2,1,0:T(2,128)S(1)}, f32[96,2,384]{2,1,0:T(2,128)}, u32[]{:S(2)}) copy-start(f32[96,2,384]{2,1,0:T(2,128)} %get-tuple-element.14) | copy-start | bytes 884740

commit v3 on v2

--- a/solution.py
+++ b/solution.py
@@ -21,7 +21,7 @@
 def kernel(cfg, fam_ref, depth_ref, x_ref, cot_ref, wq_ref, wk_ref, wv_ref, wo_ref,
            out_ref, ig_ref, wg_ref,
            xf, cf, wor, mf, igr, igs, qs, ks, vs, os_, kp, vp, gqk, gv,
-           part, xrecv, lrecv, rrecv, fsend, bsend, tsend, tfull, gpart, gxrecv,
+           part, xrecv, lrecv, rrecv, fsend, bsend, tsend, tfull, att, gpart, gxrecv,
            qfrecv, qbrecv, qfsend, qbsend, kfrecv, kbrecv, kfsend, kbsend, kxsend, kxrecv,
            h_send, h_recv, x_send, x_recv, f_send, f_recv, b_send, b_recv, t_send, t_recv,
            gx_send, gx_recv, qf_send, qf_recv, qb_send, qb_recv,
@@ -213,7 +213,8 @@
 
         return carry
 
-    lax.fori_loop(0, steps + last, chain, jnp.int32(0))
+    logits_done = n_pairs + last
+    lax.fori_loop(0, logits_done, chain, jnp.int32(0))
 
     def t_copy(k, p, d):
         return pltpu.make_async_remote_copy(
@@ -228,29 +229,43 @@
             send_sem=t_send.at[k, p, d], recv_sem=t_recv.at[k, p, d],
             device_id={"fam": fam_at(d)}, device_id_type=MESH).wait_recv()
 
-    for p in range(n_pairs):
+    def totals(s):
+        terms = row_terms(s)
+        left, right = lrecv[s], rrecv[s]
         sums = []
-        for s in (p, n_pairs + p):
-            terms = row_terms(s)
-            left, right = lrecv[s], rrecv[s]
-            for e in range(n_fam):
-                total = (has_left * same(f_prev, f_rel[e])) * left
-                total = total + (has_right * same(f_next, f_rel[e])) * right
-                for d in range(n_fam):
-                    total = total + same(f_neg[d], f_rel[e]) * terms[d]
-                sums.append(total)
+        for e in range(n_fam):
+            total = (has_left * same(f_prev, f_rel[e])) * left
+            total = total + (has_right * same(f_next, f_rel[e])) * right
+            for d in range(n_fam):
+                total = total + same(f_neg[d], f_rel[e]) * terms[d]
+            sums.append(total)
+        return sums
+
+    def give(k, p, e, value):
+        if e == 0:
+            tfull[k, p, own] = value
+        else:
+            tsend[k, p, e] = value
+            t_copy(k, p, e).start()
+
+    for p in range(n_pairs):
+        sums = totals(p)
         for e in list(range(1, n_fam)) + [0]:
             expo = jnp.exp(sums[e] * scale[e])
             attention = expo / jnp.sum(expo, axis=-1, keepdims=True)
-            grad = sums[n_fam + e]
+            att[p, e] = attention
+            give(0, p, e, attention.astype(BF16))
+        if p < last:
+            chain(logits_done + p, 0)
+    for t in range(logits_done + min(n_pairs, last), steps + last):
+        chain(t, 0)
+
+    for p in range(n_pairs):
+        sums = totals(n_pairs + p)
+        for e in list(range(1, n_fam)) + [0]:
+            attention, grad = att[p, e], sums[e]
             centred = grad - jnp.sum(attention * grad, axis=-1, keepdims=True)
-            pair = (attention.astype(BF16), (scale[e] * attention * centred).astype(BF16))
-            for k in (1, 0):
-                if e == 0:
-                    tfull[k, p, own] = pair[k]
-                else:
-                    tsend[k, p, e] = pair[k]
-                    t_copy(k, p, e).start()
+            give(1, p, e, (scale[e] * attention * centred).astype(BF16))
 
     def both(k, p):
         return jnp.concatenate([tfull[k, p, 0:cols], tfull[k, p, cols:2 * cols]], axis=1)
@@ -469,6 +484,7 @@
         vmem((steps, chunk, 128), F32), vmem((steps, chunk, 128), F32),
         vmem((steps, chunk, 128), F32), vmem((steps, chunk, 128), F32),
         vmem((2, n_pairs, n_fam, chunk, 128), BF16), vmem((2, n_pairs, 256, 128), BF16),
+        vmem((n_pairs, n_fam, chunk, 128), F32),
         vmem((2, g_all, width), BF16), vmem((g_z, n_fam, g_r, width), BF16),
         vmem((g_z, g_r, width), BF16), vmem((g_z, g_r, width), BF16),
         vmem((g_z, g_r, width), BF16), vmem((g_z, g_r, width), BF16),

time: 68 us -> 66.9 us (0.984)
  Pallas kernels: 63.5 us -> 62.4 us
    pallas_call x1, Pallas kernels: 63.5 us -> 62.4 us  [shards(): pl.pallas_call(functools.partial(kernel, cfg), out_shape=(jax.ShapeDtypeS...]
where the time goes in v3:
time: 66.9 us; the launch traced here: 66.7 us
  Pallas kernels  62.4 us (93%)
  local copies, waits for them, and re-layouts  3.65 us (5%)
    pallas_call x1, Pallas kernels, shards(): pl.pallas_call(functools.partial(kernel, cfg), out_shape=(jax.ShapeDtypeS...  62.4 us
    unnamed x7, local copies, waits for them, and re-layouts  3.65 us

profile of v3, /device:TPU:0, one launch (start us, length us, event | category | flops | bytes accessed | tf_op | source)
XLA Modules:
  0.0 66.7 jit_solution(2000176511306575400)
XLA Ops:
  0.6 62.4 %shard_map.103 = (bf16[512,384]{1,0:T(8,128)(2,1)}, bf16[512,384]{1,0:T(8,128)(2,1)}, f32[96,2,384]{2,1,0:T(2,128)}) custom-call(s32[8]{0:T(128)} %fam_ref.1, s32[4]{0:T(128)} %depth_ref.1, bf16[512,384]{1,0:T(8,128)(2,1)} %bitcast.6, bf16[512,384]{1,0:T(8,128)(2,1)} %bitcast.7, bf16[768,384]{1,0:T(8,128)(2,1)} %wq_ref.1, bf16[768,384]{1,0:T(8,128)(2,1)} %wk_ref.1, ...), custom_call_target="tpu_custom_call" | custom-call | tf_op jit(solution)/shard_map/pallas_call | solution.py:502
  63.0 0.0 copy-start
  63.0 1.8 %copy.14 = bf16[1,4,128,384]{3,2,1,0:T(8,128)(2,1)} copy(bf16[1,4,128,384]{3,2,1,0:T(8,128)(2,1)} %bitcast.5) | data formatting | bytes 786432
  64.8 0.0 copy-done
  64.9 0.0 copy-start.1
  64.9 0.7 %copy.15 = bf16[1,4,128,384]{3,2,1,0:T(8,128)(2,1)} copy(bf16[1,4,128,384]{3,2,1,0:T(8,128)(2,1)S(1)} %bitcast.4) | data formatting | bytes 786432
  65.6 0.4 copy-done.1
  66.0 0.7 %copy.16 = f32[96,2,384]{2,1,0:T(2,128)} copy(f32[96,2,384]{2,1,0:T(2,128)S(1)} %copy-done.1) | data formatting | bytes 589824
Async XLA Ops:
  63.0 1.8 %copy-start = (bf16[512,384]{1,0:T(8,128)(2,1)S(1)}, bf16[512,384]{1,0:T(8,128)(2,1)}, u32[]{:S(2)}) copy-start(bf16[512,384]{1,0:T(8,128)(2,1)} %get-tuple-element.7) | copy-start | bytes 1179652
  64.9 1.1 %copy-start.1 = (f32[96,2,384]{2,1,0:T(2,128)S(1)}, f32[96,2,384]{2,1,0:T(2,128)}, u32[]{:S(2)}) copy-start(f32[96,2,384]{2,1,0:T(2,128)} %get-tuple-element.14) | copy-start | bytes 884740

commit v4 on v3

--- a/solution.py
+++ b/solution.py
@@ -379,6 +379,16 @@
 
     for p in range(n_pairs):
         for d in range(1, n_fam):
+            t_wait(0, p, d)
+        mixed = dot(both(0, p), vs[p])
+        for r in range(rows):
+            mf[r * cols:(r + 1) * cols, pl.ds(pl.multiple_of(h * width + p * 128, 128), 128)] = (
+                mixed[:, r * 128:(r + 1) * 128].astype(BF16))
+    cm = to_head(mf.at[:, mine], mf.at[:, mine], 3)
+    cm.start()
+
+    for p in range(n_pairs):
+        for d in range(1, n_fam):
             t_wait(1, p, d)
         spread(dot(tfull[1, p], qs[p], 0, 0), gqk, width + p * 128)
     weight_part(1)
@@ -394,15 +404,6 @@
             for d in range(1, n_fam):
                 gx_copy(to_z, d).start()
 
-    for p in range(n_pairs):
-        for d in range(1, n_fam):
-            t_wait(0, p, d)
-        mixed = dot(both(0, p), vs[p])
-        for r in range(rows):
-            mf[r * cols:(r + 1) * cols, pl.ds(pl.multiple_of(h * width + p * 128, 128), 128)] = (
-                mixed[:, r * 128:(r + 1) * 128].astype(BF16))
-    cm = to_head(mf.at[:, mine], mf.at[:, mine], 3)
-    cm.start()
     k_steps(1, 2)
     for p in range(n_pairs):
         spread(dot(tfull[0, p], os_[p], 0, 0), gv, p * 128)

time: 66.9 us -> 66.9 us (level)
  no operation moved by 1% of the time
where the time goes in v4:
time: 66.9 us; the launch traced here: 66.7 us
  Pallas kernels  62.4 us (93%)
  local copies, waits for them, and re-layouts  3.65 us (5%)
    pallas_call x1, Pallas kernels, shards(): pl.pallas_call(functools.partial(kernel, cfg), out_shape=(jax.ShapeDtypeS...  62.4 us
    unnamed x7, local copies, waits for them, and re-layouts  3.65 us

profile of v4, /device:TPU:0, one launch (start us, length us, event | category | flops | bytes accessed | tf_op | source)
XLA Modules:
  0.0 66.7 jit_solution(367353805340632833)
XLA Ops:
  0.6 62.4 %shard_map.103 = (bf16[512,384]{1,0:T(8,128)(2,1)}, bf16[512,384]{1,0:T(8,128)(2,1)}, f32[96,2,384]{2,1,0:T(2,128)}) custom-call(s32[8]{0:T(128)} %fam_ref.1, s32[4]{0:T(128)} %depth_ref.1, bf16[512,384]{1,0:T(8,128)(2,1)} %bitcast.6, bf16[512,384]{1,0:T(8,128)(2,1)} %bitcast.7, bf16[768,384]{1,0:T(8,128)(2,1)} %wq_ref.1, bf16[768,384]{1,0:T(8,128)(2,1)} %wk_ref.1, ...), custom_call_target="tpu_custom_call" | custom-call | tf_op jit(solution)/shard_map/pallas_call | solution.py:503
  63.0 0.0 copy-start
  63.0 1.8 %copy.14 = bf16[1,4,128,384]{3,2,1,0:T(8,128)(2,1)} copy(bf16[1,4,128,384]{3,2,1,0:T(8,128)(2,1)} %bitcast.5) | data formatting | bytes 786432
  64.8 0.0 copy-done
  64.9 0.0 copy-start.1
  64.9 0.7 %copy.15 = bf16[1,4,128,384]{3,2,1,0:T(8,128)(2,1)} copy(bf16[1,4,128,384]{3,2,1,0:T(8,128)(2,1)S(1)} %bitcast.4) | data formatting | bytes 786432
  65.6 0.4 copy-done.1
  66.0 0.7 %copy.16 = f32[96,2,384]{2,1,0:T(2,128)} copy(f32[96,2,384]{2,1,0:T(2,128)S(1)} %copy-done.1) | data formatting | bytes 589824
Async XLA Ops:
  63.0 1.8 %copy-start = (bf16[512,384]{1,0:T(8,128)(2,1)S(1)}, bf16[512,384]{1,0:T(8,128)(2,1)}, u32[]{:S(2)}) copy-start(bf16[512,384]{1,0:T(8,128)(2,1)} %get-tuple-element.7) | copy-start | bytes 1179652
  64.9 1.1 %copy-start.1 = (f32[96,2,384]{2,1,0:T(2,128)S(1)}, f32[96,2,384]{2,1,0:T(2,128)}, u32[]{:S(2)}) copy-start(f32[96,2,384]{2,1,0:T(2,128)} %get-tuple-element.14) | copy-start | bytes 884740
